TPU v7x, 256 devices: a whole 4x4x8 slice. The times are simulated.
256 devices in a mesh: gx: 16 (over z_lo, y, core), gy: 4 (over x), grp: 4 (over z_hi).
Axes of the slice: x: 4, y: 4, z: 8 (z_hi: 4, z_lo: 2; z = z_hi * 2 + z_lo), core: 2. Of those that a mesh axis runs over, the one named last changes fastest.
Arguments:
- deflation: bfloat16 [32, 3, 128, 64, 256], P('grp', None, 'gx', 'gy'), may hold values from -3.3 to 3.3
- region: int32 [128, 64, 256], P('gx', 'gy'), may hold values from 0 to 7
- lame_table: float32 [8, 2], replicated, may hold values from 0.3 to 3
- residual: float32 [3, 128, 64, 256], P(None, 'gx', 'gy'), may hold values from -5 to 5
Outputs:
- coarse_rows: float32 [16, 4, 3, 3, 32, 32], P('gx', 'gy', None, None, 'grp')
- coarse_solution: float32 [16, 4, 32], P(None, 'gy')
- correction: float32 [3, 128, 64, 256], P(None, 'gx', 'gy', 'grp')
All inputs are finite; a program needn't handle non-finite values.
Results may differ from a plain program's by a relative error of at most 0.0003.
Values may be sent and summed in bfloat16 or wider, within the bound.
A program may use at most 128 MiB of HBM per device.

v0:
```python
import functools

import jax
import jax.numpy as jnp
from jax import lax
from jax.experimental import pallas as pl
from jax.experimental.pallas import tpu as pltpu
from jax.sharding import PartitionSpec as P

MESH = pl.DeviceIdType.MESH
F32 = jnp.float32
BF16 = jnp.bfloat16
VECS = 32
OWN = 8
PARTS = 4
COMPS = 3
CX = 8
CY = 16
CZ = 256
XQ = 4
REGIONS = 8
LINE = 16
CELLS = COMPS * CX * CY * CZ
COLUMNS = {8: 4, 4: 8, 2: 16, 1: 16}
AROUND = (4, 5, 3, 6, 2, 7, 1)
ANY = pl.BlockSpec(memory_space=pl.ANY)
VMEM = pl.BlockSpec(memory_space=pltpu.VMEM)
LIMIT = 60 * 1024 * 1024


def lanes(rows):
    return lax.broadcasted_iota(jnp.int32, (rows, 128), 1)


def roll(x, shift):
    return pltpu.roll(x, shift % 128, x.ndim - 1)


def filter_z(v, edge):
    lane = lanes(v.shape[0]) & 63
    before = jnp.where(lane == 0, edge, roll(v, 1))
    after = jnp.where(lane == 63, edge, roll(v, -1))
    return v + 0.5 * (before + after)


def halves(a, b):
    low = lanes(a.shape[0]) < 64
    return jnp.where(low, a, b)

def split(value):
    high = value.astype(BF16)
    return high, (value - high.astype(F32)).astype(BF16)


def split_rows(value):
    return jnp.concatenate(split(value), axis=0)


def dot_nt(a, b):
    return lax.dot_general(a, b, (((1,), (1,)), ((), ())), preferred_element_type=F32)


def filter_x(b):
    low = lanes(b[0].shape[0]) < 64
    zero = jnp.zeros_like(b[0])
    before = [jnp.where(low, zero, roll(b[3], 64))] + b[:3]
    after = b[1:] + [jnp.where(low, roll(b[0], 64), zero)]
    return [mid + 0.5 * (lo + hi) for mid, lo, hi in zip(b, before, after)]


def fold(a, b):
    low = lanes(a.shape[0]) < 64
    blocks = []
    for t in range(2):
        ta, tb = a[:, 128 * t : 128 * t + 128], b[:, 128 * t : 128 * t + 128]
        blocks.append(jnp.where(low, ta, roll(tb, 64)))
        blocks.append(jnp.where(low, roll(ta, 64), tb))
    return blocks


def fill_order(order):
    r = lax.broadcasted_iota(jnp.int32, (128, 128), 0)
    c = lax.broadcasted_iota(jnp.int32, (128, 128), 1)
    order[...] = jnp.where(c == (r & 7) * 16 + (r >> 3), 1.0, 0.0).astype(BF16)


def pack(k, vec, order, rows, send, edge):
    lane = lanes(8) & 63
    acc = [[jnp.zeros((8, 128), F32) for _ in range(2)] for _ in range(PARTS)]
    for xq in range(XQ):
        for half in range(2):
            plane = vec[:, k, xq + XQ * half].reshape(OWN * CY, CZ)
            rows[half] = jnp.dot(order[...], plane, preferred_element_type=F32)
        for y2 in range(CY // 2):
            both = []
            for yy in range(2):
                y = 2 * y2 + yy
                blocks = fold(rows[0, 8 * y : 8 * y + 8, :], rows[1, 8 * y : 8 * y + 8, :])
                e = 2 * (CY * (xq % 2) + y)
                for g in range(PARTS):
                    value = acc[g][xq // 2]
                    if g > 0:
                        value = jnp.where(lane == e, roll(blocks[g - 1], e + 65), value)
                    if g < PARTS - 1:
                        value = jnp.where(lane == ((e + 63) & 63), roll(blocks[g + 1], e + 63), value)
                    acc[g][xq // 2] = value
                both.append(blocks)
            for g in range(PARTS):
                send[g, k, xq, y2] = jnp.concatenate([both[0][g], both[1][g]], axis=0).astype(BF16)
    for g in range(PARTS):
        edge[g, k] = jnp.concatenate(acc[g], axis=0).astype(BF16)


def material(me, region, lame, mat):
    lane = lanes(CY) & 63
    for xq in range(XQ):
        for which in range(2):
            tiles = []
            for half in range(2):
                kind = region[xq + XQ * half]
                value = jnp.zeros((CY, CZ), F32)
                for label in range(REGIONS):
                    entry = jnp.broadcast_to(lame[which : which + 1, label : label + 1], (CY, CZ))
                    value = jnp.where(kind == label, entry, value)
                tiles.append(value)
            blocks = fold(*tiles)
            own = jnp.zeros((CY, 128), F32)
            rim = jnp.zeros((CY, 128), F32)
            for g in range(PARTS):
                here = jnp.full((CY, 128), me, jnp.int32) == g
                own = jnp.where(here, blocks[g], own)
                if which == 0 and g > 0:
                    rim = jnp.where(here & (lane == 0), roll(blocks[g - 1], 65), rim)
                if which == 0 and g < PARTS - 1:
                    rim = jnp.where(here & (lane == 63), roll(blocks[g + 1], 63), rim)
            if which == 0:
                mat[0, xq] = own
                mat[1, xq] = rim
            else:
                mat[2, xq] = own


def right_side(vec, res, rhs):
    def component(i, totals):
        k, x = i // CX, i % CX
        new = []
        for p in range(OWN):
            value = vec[p, k, x].astype(F32) * res[k, x]
            value = (value[0:8, 0:128] + value[0:8, 128:256]) + (value[8:16, 0:128] + value[8:16, 128:256])
            new.append(totals[p] + value)
        return tuple(new)

    totals = lax.fori_loop(0, COMPS * CX, component, tuple(jnp.zeros((8, 128), F32) for _ in range(OWN)))
    for p in range(OWN):
        value = jnp.sum(jnp.sum(totals[p], axis=0, keepdims=True), axis=1, keepdims=True)
        rhs[p : p + 1, :] = jnp.broadcast_to(value * (1.0 / CELLS), (1, 128))


def coefficients(live_x, live_y, mat, sx, sy, sc, se, sh, db, hb, tmp):
    for target, t in ((se, 0), (sh, 1)):
        target[...] = jnp.zeros_like(target)

        def wider(own, minus, plus):
            return roll(halves(own[3], minus), 64), roll(halves(plus, own[0]), 64)

        own = [mat[t, xq] for xq in range(XQ)]
        first, last = wider(own, sx[0, t] * live_x[0], sx[1, t] * live_x[1])
        for xq, value in enumerate([first] + own + [last]):
            target[xq, 8:24, :] = value
        for j, at, src in ((0, 7, 7), (1, 24, 0)):
            own = [sy[j, t, xq, src : src + 1, :] * live_y[j] for xq in range(XQ)]
            first, last = wider(
                own,
                sc[j, t, src : src + 1, :] * (live_x[0] * live_y[j]),
                sc[2 + j, t, src : src + 1, :] * (live_x[1] * live_y[j]),
            )
            for xq, value in enumerate([first] + own + [last]):
                target[xq, at : at + 1, :] = value
    fz = [filter_z(se[xq], sh[xq]) for xq in range(XQ + 2)]
    for xq in range(XQ):
        tmp[...] = fz[xq + 1] + 0.5 * (fz[xq] + fz[xq + 2])
        smooth = tmp[8:24, :] + 0.5 * (tmp[7:23, :] + tmp[9:25, :])
        bulk = mat[2, xq]
        db[xq] = 0.5 * (0.5 + 8.0 * mat[0, xq] + smooth + bulk)
        hb[xq] = bulk * (1.0 / 6.0)


def rows_of(ref_at, yy):
    return jnp.concatenate([ref_at(src).astype(F32)[8 * yy : 8 * yy + 8] for src in range(PARTS)], axis=0)


def prepare(k, xqs, recv, zh, zf, hz, hx, hr, hy):
    for xq in xqs:
        for y2 in range(CY // 2):
            parts = [recv[src, k, xq, y2].astype(F32) for src in range(PARTS)]
            for yy in range(2):
                y = 2 * y2 + yy
                value = jnp.concatenate([p[8 * yy : 8 * yy + 8] for p in parts], axis=0)
                zf[xq, y] = value
                e = 2 * (CY * (xq % 2) + y)
                blocks = [
                    roll(zh[src, k].astype(F32)[8 * (xq // 2) : 8 * (xq // 2) + 8], -e) for src in range(PARTS)
                ]
                around = jnp.concatenate(blocks, axis=0)
                if xq == 0:
                    hx[y] = around
                if y == 0:
                    hr[xq] = around
                hz[xq, y] = filter_z(value, around)
    for xq in xqs:
        hy[xq, 0] = 0.5 * hz[xq, 0]
        hy[xq, CY + 1] = 0.5 * hz[xq, CY - 1]
        for y in range(CY):
            sides = [hz[xq, y + d] for d in (-1, 1) if 0 <= y + d < CY]
            both = sides[0] + sides[1] if len(sides) == 2 else sides[0]
            hy[xq, y + 1] = hz[xq, y] + 0.5 * both


def combine(zf, zsum, hy, se, db, hb, wide, acc):
    for y4 in range(CY // 4):
        for y in range(4 * y4, 4 * y4 + 4):
            smooth = filter_x([hy[xq, y + 1] for xq in range(XQ)])
            for xq in range(XQ):
                v = zf[xq, y]
                before = zsum[xq, y]
                zsum[xq, y] = before + v
                w = db[xq, y : y + 1, :] * v - hb[xq, y : y + 1, :] * (v + 2.0 * before)
                w = w - se[xq + 1, y + 8 : y + 9, :] * smooth[xq]
                high, rest = split(w)
                at = 128 * (XQ * (y - 4 * y4) + xq)
                wide[0:32, at : at + 128] = high
                wide[32:64, at : at + 128] = rest
                wide[64:96, at : at + 128] = v.astype(BF16)
        acc[...] += dot_nt(wide[0:64, :], wide[64:96, :])


def row_before(k, zf, hr, hy, se, sh, ly):
    smooth = filter_x([hy[xq, 0] for xq in range(XQ)])
    scaled = []
    for xq in range(XQ):
        u = se[xq + 1, 8:9, :] * zf[xq, 0]
        scaled.append(filter_z(u, sh[xq + 1, 8:9, :] * hr[xq]))
    scaled = filter_x(scaled)
    for xq in range(XQ):
        ly[k, :, 128 * xq : 128 * xq + 128] = split_rows(-(se[xq + 1, 7:8, :] * smooth[xq] + 0.5 * scaled[xq]))


def plane_before(k, zf, hx, hy, hp, se, sh, lx, lc):
    low = lanes(VECS) < 64
    zero = jnp.zeros((VECS, 128), F32)
    for y in range(CY):
        hp[y] = filter_z(se[1, y + 8 : y + 9, :] * zf[0, y], sh[1, y + 8 : y + 9, :] * hx[y])

    def plane(y):
        if y < 0:
            second = 0.5 * hp[0]
        elif y >= CY:
            second = 0.5 * hp[CY - 1]
        else:
            sides = [hp[y + d] for d in (-1, 1) if 0 <= y + d < CY]
            second = hp[y] + 0.5 * (sides[0] + sides[1] if len(sides) == 2 else sides[0])
        return -0.5 * (se[0, y + 8 : y + 9, :] * hy[0, y + 1] + second)

    for y in range(CY // 2):
        lx[k, :, 128 * y : 128 * y + 128] = split_rows(jnp.where(low, plane(y), roll(plane(y + CY // 2), 64)))
    lc[k, 0] = split_rows(jnp.where(low, zero, roll(plane(-1), 64)))
    lc[k, 1] = split_rows(jnp.where(low, plane(CY), zero))


def both_parts(value):
    return value[0:32, :] + value[32:64, :]


def plane_products(lx, xf):
    def component(k, total):
        right = [rows_of(lambda src: xf[k, src, y // 2], y % 2).astype(BF16) for y in range(CY // 2)]
        return total + dot_nt(lx[k], jnp.concatenate(right, axis=1))

    return both_parts(lax.fori_loop(0, COMPS, component, jnp.zeros((64, 32), F32)))


def other_products(ly, lc, yf, cf):
    def component(k, sums):
        right = [rows_of(lambda src: yf[k, src, xq // 2], xq % 2).astype(BF16) for xq in range(XQ)]
        new = [dot_nt(ly[k], jnp.concatenate(right, axis=1))]
        for j, yy in ((0, 1), (1, 0)):
            new.append(dot_nt(lc[k, j], rows_of(lambda src: cf[j, k, src], yy).astype(BF16)))
        return tuple(a + b for a, b in zip(sums, new))

    sums = lax.fori_loop(0, COMPS, component, tuple(jnp.zeros((64, 32), F32) for _ in range(3)))
    return [both_parts(v) for v in sums]


def pack_plane(k, recv, xs):
    low = lanes(16) < 64
    for src in range(PARTS):
        for j in range(CY // 4):
            a = recv[src, k, 3, j].astype(F32)
            b = recv[src, k, 3, j + CY // 4].astype(F32)
            xs[k, src, j] = jnp.where(low, roll(a, 64), b).astype(BF16)


def pack_row(k, recv, ys):
    for src in range(PARTS):
        for j in range(XQ // 2):
            pair = [recv[src, k, 2 * j + i, CY // 2 - 1].astype(F32)[8:16] for i in range(2)]
            ys[k, src, j] = jnp.concatenate(pair, axis=0).astype(BF16)


SIDES = ((-1, 0), (1, 0), (0, -1), (0, 1), (-1, -1), (-1, 1), (1, -1), (1, 1))
TILE = {-1: 0, 1: 3}
ROW = {-1: 0, 1: 8}


def main_kernel(
    vec_hbm, region_hbm, lame_hbm, res_hbm, keep, line, rows,
    vec, region, lame, res, order, planes, send, edge, mat, rhs, recv, zh, xf, yf, cf, sx, sy, sc, xs, ys,
    zf, zsum, hz, hx, hr, hy, hp, se, sh, db, hb, tmp, wide, acc_c, lx, ly, lc,
    part, rest, first_in, second_in, total, corner,
    in_sem, zs, zr, hs, hv, ms, mr, own_sem, keep_sem, last_sem, s1, r1, s2, r2, s3, r3, s4, r4,
):
    gx, gy, g = lax.axis_index("gx"), lax.axis_index("gy"), lax.axis_index("grp")
    nx, ny = LINE, 4
    up, down, far = lax.rem(g + 1, 4), lax.rem(g + 3, 4), lax.rem(g + 2, 4)
    near = {}
    for dx, dy in SIDES:
        near[dx, dy] = {"gx": lax.rem(gx + dx + nx, nx), "gy": lax.rem(gy + dy + ny, ny)}

    def remote(src, dst, send_sem, recv_sem, device):
        return pltpu.make_async_remote_copy(
            src_ref=src, dst_ref=dst, send_sem=send_sem, recv_sem=recv_sem,
            device_id=device, device_id_type=MESH,
        )

    barrier = pltpu.get_barrier_semaphore()
    for other in (far, up, down):
        pl.semaphore_signal(barrier, inc=1, device_id={"grp": other}, device_id_type=MESH)
    for side in SIDES:
        if side[1] != 0:
            pl.semaphore_signal(barrier, inc=1, device_id=near[side], device_id_type=MESH)
    half, place = gx // 8, lax.rem(gx, 8)
    mates = [8 * (1 - half) + lax.rem(place + i, 8) for i in (*AROUND, 0)]
    mates += [8 * half + lax.rem(place + i, 8) for i in AROUND]
    for mate in mates:
        pl.semaphore_signal(barrier, inc=1, device_id={"gx": mate}, device_id_type=MESH)

    def load(k):
        return pltpu.make_async_copy(vec_hbm.at[:, k], vec.at[:, k], in_sem.at[k])

    loads = [
        pltpu.make_async_copy(region_hbm, region, in_sem.at[3]),
        pltpu.make_async_copy(lame_hbm, lame, in_sem.at[4]),
        pltpu.make_async_copy(res_hbm, res, in_sem.at[5]),
    ]
    for k in range(COMPS):
        load(k).start()
    for c in loads:
        c.start()
    fill_order(order)

    def zcopy(src, dst, kind, k, other):
        return remote(src, dst, zs.at[kind, k], zr.at[kind, k], {"grp": other})

    def ahead(k):
        last = pl.ds(XQ - 1, 1)
        return [zcopy(send.at[o, k, last], recv.at[g, k, last], i, k, o) for i, o in enumerate((far, up, down))]

    def second(k):
        part = pl.ds(0, 2)
        return [zcopy(send.at[o, k, part], recv.at[g, k, part], 3 + i, k, o) for i, o in enumerate((far, up, down))]

    def third(k):
        part = pl.ds(2, 1)
        return [zcopy(send.at[o, k, part], recv.at[g, k, part], 9 + i, k, o) for i, o in enumerate((far, up, down))]

    def edges(k):
        return [zcopy(edge.at[o, k], zh.at[g, k], 6 + i, k, o) for i, o in enumerate((far, up, down))]

    def own(k):
        return [
            pltpu.make_async_copy(send.at[g, k], recv.at[g, k], own_sem.at[0, k]),
            pltpu.make_async_copy(edge.at[g, k], zh.at[g, k], own_sem.at[1, k]),
        ]

    def start(copies):
        for c in copies:
            c.start()

    load(0).wait()
    pack(0, vec, order, planes, send, edge)
    pl.semaphore_wait(barrier, 3 + 6 + nx - 1)
    start(ahead(0) + edges(0) + second(0) + third(0) + own(0))

    def pack_more(k, _):
        load(k).wait()
        pack(k, vec, order, planes, send, edge)
        start(ahead(k) + edges(k) + own(k))
        return 0

    lax.fori_loop(1, COMPS, pack_more, 0)
    for c in loads:
        c.wait()
    material(g, region, lame, mat)
    mats = []

    def mcopy(src, dst, side):
        i = len(mats)
        mats.append(remote(src, dst, ms.at[i], mr.at[i], near[side]))

    for dx in (-1, 1):
        mcopy(mat.at[pl.ds(0, 2), TILE[dx]], sx.at[1 if dx < 0 else 0], (dx, 0))
    for dy in (-1, 1):
        mcopy(mat.at[pl.ds(0, 2), :, pl.ds(ROW[dy], 8)], sy.at[1 if dy < 0 else 0], (0, dy))
    for dx in (-1, 1):
        for dy in (-1, 1):
            slot = (2 if dx < 0 else 0) + (1 if dy < 0 else 0)
            mcopy(mat.at[pl.ds(0, 2), TILE[dx], pl.ds(ROW[dy], 8)], sc.at[slot], (dx, dy))
    for c in mats:
        c.start()
    right_side(vec, res, rhs)
    for c in mats:
        c.wait_recv()
    one = jnp.ones((1, 128), F32)
    none = jnp.zeros((1, 128), F32)
    live_x = (jnp.where(gx > 0, one, none), jnp.where(gx < nx - 1, one, none))
    live_y = (jnp.where(gy > 0, one, none), jnp.where(gy < ny - 1, one, none))
    coefficients(live_x, live_y, mat, sx, sy, sc, se, sh, db, hb, tmp)
    for ref in (zsum, acc_c):
        ref[...] = jnp.zeros_like(ref)

    def hcopy(a, b, i, k, side):
        return remote(a, b, hs.at[k, i], hv.at[k, i], near[side])

    def early(k):
        return [hcopy(xs.at[k], xf.at[k], 0, k, (1, 0))]

    def corners(k):
        return [
            hcopy(xf.at[k, :, 3], cf.at[0, k], 1, k, (0, 1)),
            hcopy(xf.at[k, :, 0], cf.at[1, k], 2, k, (0, -1)),
        ]

    def late(k):
        return [hcopy(ys.at[k], yf.at[k], 3, k, (0, 1))]

    def planes_first(k, _):
        for c in own(k):
            c.wait()
        for c in ahead(k):
            c.wait_recv()
        pack_plane(k, recv, xs)
        start(early(k))
        return 0

    scale = 1.0 / CELLS
    mine = pl.ds(pl.multiple_of(8 * g, 8), 8)
    planes_first(0, 0)

    def component(k, _):
        for c in second(k) + edges(k):
            c.wait_recv()
        prepare(k, (3, 0, 1), recv, zh, zf, hz, hx, hr, hy)
        plane_before(k, zf, hx, hy, hp, se, sh, lx, lc)

        @pl.when(k == 0)
        def _():
            start(second(1))
            lax.fori_loop(1, COMPS, planes_first, 0)
            start(third(1) + second(2) + third(2))

        @pl.when(k == 1)
        def _():
            for i in range(COMPS):
                early(i)[0].wait_recv()
                start(corners(i))

        @pl.when(k == COMPS - 1)
        def _():
            lower = plane_products(lx, xf) * (scale * live_x[0][:, 0:32])
            part[...] = jnp.zeros_like(part)
            part[:, 32:64] = lower
            part[:, 64:96] = lower.T
            part[mine, 96:128] = rhs[:, 0:32]

        for c in third(k):
            c.wait_recv()
        pack_row(k, recv, ys)
        start(late(k))
        pltpu.make_async_copy(recv.at[:, k], keep.at[:, k], keep_sem.at[k]).start()
        prepare(k, (2,), recv, zh, zf, hz, hx, hr, hy)
        combine(zf, zsum, hy, se, db, hb, wide, acc_c)

        @pl.when(k < COMPS - 1)
        def _():
            row_before(k, zf, hr, hy, se, sh, ly)

        return 0

    lax.fori_loop(0, COMPS, component, 0)

    inner = both_parts(acc_c[...])
    part[:, 0:32] = (inner + inner.T) * scale

    sums = []
    for i, other in enumerate((far, up, down)):
        sums.append(remote(part, first_in.at[g], s1.at[i], r1.at[i], {"grp": other}))
    start(sums)
    row_before(COMPS - 1, zf, hr, hy, se, sh, ly)
    for k in range(COMPS):
        for c in corners(k) + late(k):
            c.wait_recv()
    side, *diagonal = other_products(ly, lc, yf, cf)
    side = side * (scale * live_y[0][:, 0:32])
    rest[...] = jnp.zeros_like(rest)
    rest[:, 0:32] = side
    rest[:, 128:160] = side.T
    for j in range(2):
        value = diagonal[j] * (scale * (live_x[0] * live_y[j])[:, 0:32])
        rest[:, 32 + 32 * j : 64 + 32 * j] = value
        rest[:, 160 + 32 * j : 192 + 32 * j] = value.T
    for i, other in enumerate((far, up, down)):
        theirs = pl.ds(pl.multiple_of(8 * other, 8), 8)
        sums.append(remote(rest.at[theirs], second_in.at[g], s2.at[i], r2.at[i], {"grp": other}))
    start(sums[3:])
    first_in[pl.ds(g, 1)] = part[...].reshape(1, VECS, 128)
    second_in[pl.ds(g, 1)] = rest[mine, :].reshape(1, 8, 256)
    for c in sums[:3]:
        c.wait_recv()
    total[...] = (first_in[0] + first_in[1]) + (first_in[2] + first_in[3])
    sends = []
    for i, mate in enumerate(mates):
        c = remote(total, line.at[gx], s3.at[i], r3.at[i], {"gx": mate})
        c.start()
        sends.append(c)
    kept = [
        pltpu.make_async_copy(total, line.at[gx], last_sem.at[0]),
        pltpu.make_async_copy(total.at[mine], rows.at[0], last_sem.at[1]),
        pltpu.make_async_copy(corner.at[0], rows.at[1], last_sem.at[2]),
    ]
    start(kept[:2])
    for c in sums[3:]:
        c.wait_recv()
    both = (second_in[0] + second_in[1]) + (second_in[2] + second_in[3])
    corner[0] = both[:, 0:128]
    corner[1] = both[:, 128:256]
    start(kept[2:])
    for i, to in enumerate(((0, -1), (-1, -1), (-1, 1))):
        c = remote(corner.at[1], rows.at[2 + i], s4.at[i], r4.at[i], near[to])
        c.start()
        sends.append(c)

    def finish(k, _):
        for c in ahead(k) + second(k) + third(k) + edges(k) + early(k) + corners(k) + late(k):
            c.wait_send()
        pltpu.make_async_copy(recv.at[:, k], keep.at[:, k], keep_sem.at[k]).wait()
        return 0

    lax.fori_loop(0, COMPS, finish, 0)
    for c in mats + sums:
        c.wait_send()
    for c in kept:
        c.wait()
    for c in sends:
        c.wait_recv()
    for c in sends:
        c.wait_send()


def main(deflation, region, lame_table, residual):
    field = (XQ, CY, VECS, 128)
    packed = (PARTS, COMPS, XQ, CY // 2, 16, 128)
    dma = pltpu.SemaphoreType.DMA
    return pl.pallas_call(
        main_kernel,
        name="main",
        out_shape=(
            jax.ShapeDtypeStruct(packed, BF16),
            jax.ShapeDtypeStruct((LINE, VECS, 128), F32),
            jax.ShapeDtypeStruct((5, 8, 128), F32),
        ),
        in_specs=[ANY] * 4,
        out_specs=[ANY, ANY, ANY],
        scratch_shapes=[
            pltpu.VMEM((OWN, COMPS, CX, CY, CZ), BF16),
            pltpu.VMEM((CX, CY, CZ), jnp.int32),
            pltpu.VMEM((2, REGIONS), F32),
            pltpu.VMEM((COMPS, CX, CY, CZ), F32),
            pltpu.VMEM((128, 128), BF16),
            pltpu.VMEM((2, 128, 256), F32),
            pltpu.VMEM(packed, BF16),
            pltpu.VMEM((PARTS, COMPS, 16, 128), BF16),
            pltpu.VMEM((3, XQ, CY, 128), F32),
            pltpu.VMEM((8, 128), F32),
            pltpu.VMEM(packed, BF16),
            pltpu.VMEM((PARTS, COMPS, 16, 128), BF16),
            pltpu.VMEM((COMPS, PARTS, CY // 4, 16, 128), BF16),
            pltpu.VMEM((COMPS, PARTS, XQ // 2, 16, 128), BF16),
            pltpu.VMEM((2, COMPS, PARTS, 16, 128), BF16),
            pltpu.VMEM((2, 2, CY, 128), F32),
            pltpu.VMEM((2, 2, XQ, 8, 128), F32),
            pltpu.VMEM((4, 2, 8, 128), F32),
            pltpu.VMEM((COMPS, PARTS, CY // 4, 16, 128), BF16),
            pltpu.VMEM((COMPS, PARTS, XQ // 2, 16, 128), BF16),
            pltpu.VMEM(field, F32),
            pltpu.VMEM(field, F32),
            pltpu.VMEM(field, F32),
            pltpu.VMEM((CY, VECS, 128), F32),
            pltpu.VMEM((XQ, VECS, 128), F32),
            pltpu.VMEM((XQ, CY + 2, VECS, 128), F32),
            pltpu.VMEM((CY, VECS, 128), F32),
            pltpu.VMEM((XQ + 2, 32, 128), F32),
            pltpu.VMEM((XQ + 2, 32, 128), F32),
            pltpu.VMEM((XQ, CY, 128), F32),
            pltpu.VMEM((XQ, CY, 128), F32),
            pltpu.VMEM((32, 128), F32),
            pltpu.VMEM((96, 2048), BF16),
            pltpu.VMEM((64, 32), F32),
            pltpu.VMEM((COMPS, 64, 1024), BF16),
            pltpu.VMEM((COMPS, 64, 512), BF16),
            pltpu.VMEM((COMPS, 2, 64, 128), BF16),
            pltpu.VMEM((VECS, 128), F32),
            pltpu.VMEM((VECS, 256), F32),
            pltpu.VMEM((PARTS, VECS, 128), F32),
            pltpu.VMEM((PARTS, 8, 256), F32),
            pltpu.VMEM((VECS, 128), F32),
            pltpu.VMEM((2, 8, 128), F32),
            dma((6,)),
            dma((12, COMPS)),
            dma((12, COMPS)),
            dma((COMPS, 4)),
            dma((COMPS, 4)),
            dma((8,)),
            dma((8,)),
            dma((2, COMPS)),
            dma((COMPS,)),
            dma((3,)),
            dma((3,)),
            dma((3,)),
            dma((3,)),
            dma((3,)),
            dma((LINE - 1,)),
            dma((LINE - 1,)),
            dma((3,)),
            dma((3,)),
        ],
        compiler_params=pltpu.CompilerParams(
            vmem_limit_bytes=LIMIT, collective_id=0, has_side_effects=True
        ),
    )(deflation, region, lame_table, residual)


def eliminate(blocks):
    step = COLUMNS[len(blocks)]
    m = [jnp.stack([b[8 * i : 8 * i + 8] for b in blocks]) for i in range(4)]
    sub = lax.broadcasted_iota(jnp.int32, m[0].shape, 1)

    def take(x, column, j, pivot):
        new = []
        for i in range(4):
            value = x[i] - column[i] * pivot
            new.append(jnp.where(sub == j % 8, pivot, value) if i == j // 8 else value)
        return new

    for start in range(0, VECS, step):
        columns = [[jnp.broadcast_to(x[:, :, j : j + 1], x.shape) for x in m] for j in range(start, start + step)]
        for i in range(step):
            j = start + i
            at, row = j // 8, j % 8
            column = columns[i]
            inverse = 1.0 / column[at][:, row : row + 1, :]
            for other in range(i + 1, step):
                pivot = columns[other][at][:, row : row + 1, :] * inverse
                columns[other] = take(columns[other], column, j, pivot)
            m = take(m, column, j, m[at][:, row : row + 1, :] * inverse)
    return [jnp.concatenate([m[i][b] for i in range(4)], axis=0) for b in range(len(blocks))]


def solve_kernel(line, rows, keep, blocks, solved, corr, recv, table, weights, corr_rows, sem):
    fetch = pltpu.make_async_copy(keep, recv, sem.at[0])
    fetch.start()
    gx, g = lax.axis_index("gx"), lax.axis_index("grp")
    lane = lanes(VECS)
    sub = lax.broadcasted_iota(jnp.int32, (VECS, 128), 0)

    def reduce_level(system):
        odd = eliminate(system[1::2])
        rest = []
        for i, m in enumerate(system[0::2]):
            coeff = roll(m, -32)[:, 0:64]
            if i > 0:
                b = odd[i - 1]
                left = jnp.where(lane < 32, roll(b, 64), jnp.where((lane >= 64) & (lane < 96), 0.0, b))
            else:
                left = jnp.zeros((VECS, 128), F32)
            b = odd[i]
            right = jnp.where(lane < 32, roll(b, -32), jnp.where((lane >= 32) & (lane < 64), 0.0, b))
            change = lax.dot_general(
                coeff, jnp.concatenate([left, right], axis=0), (((1,), (0,)), ((), ())),
                precision=lax.Precision.HIGHEST, preferred_element_type=F32)
            rest.append(jnp.where((lane >= 32) & (lane < 96), 0.0, m) - change)
        return odd, rest

    levels = []
    after = (lane >= 64) & (lane < 96)
    system = [jnp.where(after, line[(a + 1) % LINE], line[a]) for a in range(LINE)]
    while len(system) > 1:
        odd, system = reduce_level(system)
        levels.append(odd)
    last = eliminate(system)[0]

    def spread(column):
        return jnp.broadcast_to(column, (VECS, 128))

    def as_row(full, shift):
        return jnp.sum(jnp.where(lane == sub + shift, full, 0.0), axis=0, keepdims=True)

    values = [spread(last[:, 96:97])]
    for odd in reversed(levels):
        new = []
        for i, m in enumerate(odd):
            row = as_row(values[i], 32)
            if i + 1 < len(values):
                row = row + as_row(values[i + 1], 64)
            picked = jnp.where(lane == 96, m, jnp.where((lane >= 32) & (lane < 96), -m * row, 0.0))
            new.append(spread(jnp.sum(picked, axis=1, keepdims=True)))
        values = [v for pair in zip(values, new) for v in pair]
    for a in range(LINE):
        table[a] = values[a]
        solved[a : a + 1, :] = as_row(values[a], 0)[:, 0:32]

    weights[...] = table[gx]
    fetch.wait()

    def component(k, _):
        for xq in range(XQ):
            for y2 in range(CY // 2):
                even = jnp.zeros((8, 128), F32)
                odd = jnp.zeros((8, 128), F32)
                for src in range(PARTS):
                    v = recv[src, k, xq, y2].astype(F32)
                    w = weights[8 * src : 8 * src + 8, :]
                    even = even + w * v[:8]
                    odd = odd + w * v[8:]
                corr_rows[2 * y2 : 2 * y2 + 1, :] = jnp.sum(even, axis=0, keepdims=True)
                corr_rows[2 * y2 + 1 : 2 * y2 + 2, :] = jnp.sum(odd, axis=0, keepdims=True)
            whole = corr_rows[...]
            corr[k, xq] = whole[:, 0:64]
            corr[k, xq + XQ] = roll(whole, 64)[:, 0:64]
        return 0

    lax.fori_loop(0, COMPS, component, 0)
    mine = pl.ds(pl.multiple_of(8 * g, 8), 8)
    blocks[1, 1] = rows[0, :, 0:32]
    blocks[0, 1] = rows[0, :, 32:64]
    blocks[2, 1] = line[lax.rem(gx + 1, LINE), mine, :][:, 64:96]
    blocks[1, 0] = rows[1, :, 0:32]
    blocks[0, 0] = rows[1, :, 32:64]
    blocks[0, 2] = rows[1, :, 64:96]
    blocks[1, 2] = rows[2, :, 0:32]
    blocks[2, 2] = rows[3, :, 32:64]
    blocks[2, 0] = rows[4, :, 64:96]


def solve(line, rows, keep):
    return pl.pallas_call(
        solve_kernel,
        name="solve",
        out_shape=(
            jax.ShapeDtypeStruct((3, 3, OWN, VECS), F32),
            jax.ShapeDtypeStruct((LINE, VECS), F32),
            jax.ShapeDtypeStruct((COMPS, CX, CY, CZ // PARTS), F32),
        ),
        in_specs=[VMEM, VMEM, ANY],
        out_specs=[VMEM] * 3,
        scratch_shapes=[
            pltpu.VMEM((PARTS, COMPS, XQ, CY // 2, 16, 128), BF16),
            pltpu.VMEM((LINE, VECS, 128), F32),
            pltpu.VMEM((VECS, 128), F32),
            pltpu.VMEM((CY, 128), F32),
            pltpu.SemaphoreType.DMA((1,)),
        ],
        compiler_params=pltpu.CompilerParams(vmem_limit_bytes=LIMIT),
    )(line, rows, keep)


def on_device(deflation, region, lame_table, residual):
    keep, line, rows = main(deflation, region, lame_table.T, residual)
    blocks, solved, corr = solve(line, rows, keep)
    return blocks[None, None], solved[:, None, :], corr


def solution(mesh):
    placed = (P("grp", None, "gx", "gy", None), P("gx", "gy", None), P(), P(None, "gx", "gy", None))
    return jax.shard_map(
        on_device,
        mesh=mesh,
        in_specs=placed,
        out_specs=(
            P("gx", "gy", None, None, "grp", None),
            P(None, "gy", None),
            P(None, "gx", "gy", "grp"),
        ),
        check_vma=False,
    )
```

profile of v0, /device:TPU:25, one launch (start us, length us, event | category | flops | bytes accessed | tf_op | source)
XLA Modules:
  0.0 72.2 jit_solution(8375428078692203440)
XLA Ops:
  0.6 62.0 %main.1 = (bf16[4,3,4,8,16,128]{5,4,3,2,1,0:T(8,128)(2,1)}, f32[16,32,128]{2,1,0:T(8,128)}, f32[5,8,128]{2,1,0:T(8,128)}) custom-call(bf16[8,3,8,16,256]{4,3,2,1,0:T(8,128)(2,1)} %vec_hbm.1, s32[8,16,256]{2,1,0:T(8,128)} %region_hbm.1, f32[2,8]{1,0:T(2,128)} %bitcast.5, f32[3,8,16,256]{3,2,1,0:T(8,128)} %res_hbm.1), custom_call_target="tpu_custom_call" | custom-call | tf_op jit(solution)/shard_map/main/pallas_call | solution.py:573
  62.6 9.6 %solve.1 = (f32[3,3,8,32]{3,2,1,0:T(8,128)}, f32[16,32]{1,0:T(8,128)}, f32[3,8,16,64]{3,2,1,0:T(8,128)}) custom-call(f32[16,32,128]{2,1,0:T(8,128)} %get-tuple-element.9.line, f32[5,8,128]{2,1,0:T(8,128)} %get-tuple-element.10.rows, bf16[4,3,4,8,16,128]{5,4,3,2,1,0:T(8,128)(2,1)} %get-tuple-element.11.keep), custom_call_target="tpu_custom_call" | custom-call | tf_op jit(solution)/shard_map/solve/pallas_call | solution.py:765
where the time goes:
time: 72.3 us; the launch traced here: 72.2 us
  Pallas kernels  71.6 us (99%)
    pallas_call x1, Pallas kernels, main(): pl.pallas_call(main_kernel, name='main', out_shape=(jax.ShapeDtypeStruct(...  62 us
    pallas_call x1, Pallas kernels, solve(): pl.pallas_call(solve_kernel, name='solve', out_shape=(jax.ShapeDtypeStruc...  9.57 us

commit v1 on v0

--- a/solution.py
+++ b/solution.py
@@ -486,7 +486,6 @@
             c.wait_recv()
         pack_row(k, recv, ys)
         start(late(k))
-        pltpu.make_async_copy(recv.at[:, k], keep.at[:, k], keep_sem.at[k]).start()
         prepare(k, (2,), recv, zh, zf, hz, hx, hr, hy)
         combine(zf, zsum, hy, se, db, hb, wide, acc_c)
 
@@ -538,6 +537,7 @@
         pltpu.make_async_copy(corner.at[0], rows.at[1], last_sem.at[2]),
     ]
     start(kept[:2])
+    start(pltpu.make_async_copy(recv.at[:, k], keep.at[:, k], keep_sem.at[k]) for k in range(COMPS))
     for c in sums[3:]:
         c.wait_recv()
     both = (second_in[0] + second_in[1]) + (second_in[2] + second_in[3])

time: 72.3 us -> 72.3 us (level)
  no operation moved by 1% of the time
where the time goes in v1:
time: 72.3 us; the launch traced here: 72.2 us
  Pallas kernels  71.6 us (99%)
    pallas_call x1, Pallas kernels, main(): pl.pallas_call(main_kernel, name='main', out_shape=(jax.ShapeDtypeStruct(...  62 us
    pallas_call x1, Pallas kernels, solve(): pl.pallas_call(solve_kernel, name='solve', out_shape=(jax.ShapeDtypeStruc...  9.57 us

profile of v1, /device:TPU:25, one launch (start us, length us, event | category | flops | bytes accessed | tf_op | source)
XLA Modules:
  0.0 72.2 jit_solution(2345968274395109148)
XLA Ops:
  0.6 62.0 %main.1 = (bf16[4,3,4,8,16,128]{5,4,3,2,1,0:T(8,128)(2,1)}, f32[16,32,128]{2,1,0:T(8,128)}, f32[5,8,128]{2,1,0:T(8,128)}) custom-call(bf16[8,3,8,16,256]{4,3,2,1,0:T(8,128)(2,1)} %vec_hbm.1, s32[8,16,256]{2,1,0:T(8,128)} %region_hbm.1, f32[2,8]{1,0:T(2,128)} %bitcast.5, f32[3,8,16,256]{3,2,1,0:T(8,128)} %res_hbm.1), custom_call_target="tpu_custom_call" | custom-call | tf_op jit(solution)/shard_map/main/pallas_call | solution.py:573
  62.6 9.6 %solve.1 = (f32[3,3,8,32]{3,2,1,0:T(8,128)}, f32[16,32]{1,0:T(8,128)}, f32[3,8,16,64]{3,2,1,0:T(8,128)}) custom-call(f32[16,32,128]{2,1,0:T(8,128)} %get-tuple-element.9.line, f32[5,8,128]{2,1,0:T(8,128)} %get-tuple-element.10.rows, bf16[4,3,4,8,16,128]{5,4,3,2,1,0:T(8,128)(2,1)} %get-tuple-element.11.keep), custom_call_target="tpu_custom_call" | custom-call | tf_op jit(solution)/shard_map/solve/pallas_call | solution.py:765
